TPU v7x, 32 devices: a whole 2x2x4 slice. The times are simulated.
32 devices in a mesh: comp: 8 (over y, x, core), pair: 4 (over z).
Axes of the slice: x: 2, y: 2, z: 4, core: 2. Of those that a mesh axis runs over, the one named last changes fastest.
Arguments:
- densities: bfloat16 [8192, 16384], P('comp', 'pair'), may hold values from -6 to 6
- coulomb: float32 [8192], replicated, may hold values from 3.314563e-05 to 0.003314563
- pair_list: int32 [256, 2], P(('comp', 'pair')), may hold values from 0 to 4095
- valence_energy: float32 [4096], replicated, may hold values from -20 to -0.5, as said below
- conduction_energy: float32 [4096], replicated, may hold values from 0.5 to 12, as said below
- tile_mask: int32 [128, 8], P(('pair', 'comp')), may hold values 0 or 1
Outputs:
- kernel: float32 [16384, 256], P(('pair', 'comp'))
Inputs may be any that keep to these rules, and one draw needn't show every extreme that they name: `valence_energy`: energies in electronvolts. `conduction_energy`: energies in electronvolts.
All inputs are finite; a program needn't handle non-finite values. No bound on the sum of `tile_mask` on one device may be relied on, other than what follows from the above.
Results may differ from a plain program's by a relative error of at most 0.0025.
Values may be sent and summed in bfloat16 or wider, within the bound.
A program may use at most 128 MiB of HBM per device.

v0:
```python
import jax
import jax.numpy as jnp
from jax import lax
from jax.sharding import PartitionSpec as P

TILE = 128


def per_device(densities, coulomb, pair_list, valence_energy, conduction_energy, tile_mask):
    comp_count = lax.axis_size("comp")
    pair_count = lax.axis_size("pair")
    comp_index = lax.axis_index("comp")
    pair_index = lax.axis_index("pair")
    block_len = densities.shape[0]
    pair_dev = densities.shape[1] // comp_count
    row_dev = pair_list.shape[0]
    window = row_dev * comp_count * pair_count
    weights = lax.dynamic_slice_in_dim(coulomb, comp_index * block_len, block_len)
    picked = densities.reshape(block_len, comp_count, pair_dev)[:, :, :row_dev]
    local_panel = (jnp.transpose(picked, (1, 2, 0)).astype(jnp.float32) * weights).astype(
        jnp.bfloat16
    )
    gathered = lax.all_gather(local_panel, "pair", axis=1, tiled=True)
    panel = gathered.reshape(window, block_len)
    exchange = lax.psum_scatter(
        lax.dot_general(
            densities, panel, (((0,), (1,)), ((), ())), preferred_element_type=jnp.float32
        ),
        "comp",
        scatter_dimension=0,
        tiled=True,
    )
    masked = (
        exchange.reshape(pair_dev // TILE, TILE, comp_count, window // comp_count)
        * tile_mask.astype(jnp.float32)[:, None, :, None]
    )
    masked = 2.0 * masked.reshape(pair_dev, window)
    table = jnp.arange(valence_energy.shape[0], dtype=jnp.int32)
    cond_hits = pair_list[:, 1][:, None] == table[None, :]
    val_hits = pair_list[:, 0][:, None] == table[None, :]
    energy = jnp.sum(jnp.where(cond_hits, conduction_energy[None, :], 0.0), axis=1) - jnp.sum(
        jnp.where(val_hits, valence_energy[None, :], 0.0), axis=1
    )
    diag_block = jnp.eye(row_dev, dtype=jnp.float32) * energy[None, :]
    start = (comp_index * pair_count + pair_index) * row_dev
    placed = lax.dynamic_update_slice(
        jnp.zeros((pair_dev, window), jnp.float32), diag_block, (jnp.int32(0), start)
    )
    return masked + placed


def solution(mesh):
    return jax.shard_map(
        per_device,
        mesh=mesh,
        in_specs=(
            P("comp", "pair"),
            P(),
            P(("comp", "pair"), None),
            P(),
            P(),
            P(("pair", "comp"), None),
        ),
        out_specs=P(("pair", "comp"), None),
        check_vma=False,
    )
```

profile of v0, /device:TPU:0, one launch (start us, length us, event | category | flops | bytes accessed | tf_op | source)
XLA Modules:
  0.0 108.1 jit_solution(17260604384585832690)
XLA Ops:
  6.5 0.0 reduce-scatter.2.cloned.1.call-start
  6.5 12.0 %copy.12 = bf16[1024,4096]{0,1:T(8,128)(2,1)} copy(bf16[1024,4096]{1,0:T(8,128)(2,1)} %param.6) | data formatting | bytes 16777216 | tf_op args[0]
  18.5 0.7 dynamic_slice.3
  19.2 0.9 fusion.1
  20.1 17.4 %all_gather.3 = bf16[8,32,1024]{2,1,0:T(8,128)(2,1)S(1)} all-gather(bf16[8,8,1024]{2,1,0:T(8,128)(2,1)S(1)} %fusion.1), channel_id=1, replica_groups=mesh['comp'=8,'pair'=4] {'pair'}, dimensions={1}, use_global_device_ids=true | all-gather | bytes 655360 | tf_op jit(solution)/shard_map/all_gather | solution.py:23
  37.5 0.0 copy-start.2
  37.5 0.0 copy-start.3
  37.5 0.0 copy-start
  37.5 0.0 copy-start.1
  37.5 7.7 %convolution_bitcast_fusion = f32[4096,256]{0,1:T(8,128)} fusion(bf16[256,1024]{1,0:T(8,128)(2,1)S(1)} %bitcast.22, bf16[1024,4096]{1,0:T(8,128)(2,1)} %param.6), kind=kOutput, calls=%fused_computation | convolution fusion | flops 2147483648 | bytes 13107200 | tf_op jit(solution)/shard_map/dot_general | solution.py:26
  45.2 0.0 reduce-scatter.2.cloned.1.call-update
  45.2 0.0 copy-done.2
  45.3 0.1 copy.13
  45.3 0.0 copy-done.3
  45.4 0.0 copy-done
  45.4 0.0 copy-done.1
  45.4 0.2 select_reduce_fusion
  45.6 52.8 %reduce-scatter.2.cloned.1.call-done = f32[512,256]{0,1:T(8,128)} async-done(((f32[4096,256]{0,1:T(8,128)}), f32[512,256]{0,1:T(8,128)}) %reduce-scatter.2.cloned.1.call-update) | async-done | bytes 524304 | tf_op jit(solution)/shard_map/reduce_scatter | solution.py:25
  98.5 0.1 mul.48
  98.6 1.1 %fusion = f32[512,256]{0,1:T(8,128)S(1)} fusion(f32[512,256]{0,1:T(8,128)} %reduce-scatter.2.cloned.1.call-done, f32[32,8,4,128]{3,2,1,0:T(4,128)S(1)} %bitcast.21), kind=kLoop, calls=%fused_computation.2 | loop fusion | flops 262144 | bytes 1572864 | tf_op jit(solution)/shard_map/mul | solution.py:37
  99.8 0.1 select_add_fusion
  99.8 0.5 add.18
  100.3 1.0 copy.14
  (3 shorter events, 0.0 us)
Async XLA Ops:
  6.5 91.9 %reduce-scatter.2.cloned.1.call-start = ((), (), s32[]{:S(2)}) async-start(), calls=%async_computation.1 | async-start | bytes 4718592 | tf_op jit(solution)/shard_map/reduce_scatter | solution.py:25
  37.5 7.8 %copy-start.2 = (s32[4,8]{1,0:T(4,128)S(1)}, s32[4,8]{1,0:T(4,128)}, u32[]{:S(2)}) copy-start(s32[4,8]{1,0:T(4,128)} %param.11) | copy-start | bytes 388
  37.5 7.9 %copy-start.3 = (s32[8,2]{0,1:T(2,128)S(1)}, s32[8,2]{0,1:T(2,128)}, u32[]{:S(2)}) copy-start(s32[8,2]{0,1:T(2,128)} %param.8) | copy-start | bytes 196
  37.5 7.9 %copy-start = (f32[4096]{0:T(1024)S(1)}, f32[4096]{0:T(1024)}, u32[]{:S(2)}) copy-start(f32[4096]{0:T(1024)} %param.9) | copy-start | bytes 49156
  37.5 7.9 %copy-start.1 = (f32[4096]{0:T(1024)S(1)}, f32[4096]{0:T(1024)}, u32[]{:S(2)}) copy-start(f32[4096]{0:T(1024)} %param.10) | copy-start | bytes 49156
Sparse Core Ops, SparseCore 0:
  45.4 53.0 reduce-scatter.1
where the time goes:
time: 109 us; the launch traced here: 108 us
  waiting for transfers between devices  52.9 us (49%)
  blocking collectives  17.4 us (16%)
  local copies, waits for them, and re-layouts  14.4 us (13%)
  between operations  13.5 us (12%)
  matrix products  7.71 us (7%)
  other arithmetic  2.39 us (2%)
    reduce_scatter x1, waiting for transfers between devices, per_device(): lax.psum_scatter(lax.dot_general(densities, panel, (((0,), (1,)), ((), ()...  52.8 us
    all_gather x1, blocking collectives, per_device(): gathered = lax.all_gather(local_panel, 'pair', axis=1, tiled=True)  17.4 us
    unnamed x9, local copies, waits for them, and re-layouts  12 us
    dot_general x1, matrix products, per_device(): lax.dot_general(densities, panel, (((0,), (1,)), ((), ())), preferred_ele...  7.71 us
  transfers between devices with their start and end apart: 1, of which 1 were waited for; matrix products, arithmetic and copies ran while one was open for 0% of the time, Pallas kernels for 0%

commit v1 on v0

v1 whole, which is shorter than its diff:
```python
import functools

import jax
import jax.numpy as jnp
from jax import lax
from jax.experimental import pallas as pl
from jax.experimental.pallas import tpu as pltpu
from jax.sharding import PartitionSpec as P

TILE = 128
LANES = 128
MESH = pl.DeviceIdType.MESH
F32 = jnp.float32
BF16 = jnp.bfloat16


def xor(a, b, bits):
    out = 0
    for i in range(bits):
        x, y = (a // 2**i) % 2, (b // 2**i) % 2
        out = out + 2**i * (x + y - 2 * x * y)
    return out


def kernel(
    comps, pairs, row_dev,
    d_hbm, w_ref, list_ref, val_ref, cond_ref, mask_ref, out_ref,
    d_v, panel, own, core_out, core_in, chip_out, chip_in, acc,
    load_sem, pan_s, pan_r, core_s, core_r, chip_s, chip_r,
):
    c = lax.axis_index("comp")
    p = lax.axis_index("pair")
    chips = comps // 2
    chip_bits = chips.bit_length() - 1
    pair_bits = pairs.bit_length() - 1
    core, chip = c % 2, c // 2
    block_len = d_v.shape[0]
    width = d_v.shape[1] // comps
    rows = comps * row_dev
    window = pairs * rows

    def chip_at(m):
        return xor(chip, m, chip_bits)

    spans = [(b * width, LANES) for b in range(comps)]
    spans += [(b * width + LANES, width - LANES) for b in range(comps)]
    loads = [
        pltpu.make_async_copy(
            d_hbm.at[:, pl.ds(at, size)], d_v.at[:, pl.ds(at, size)], load_sem.at[i]
        )
        for i, (at, size) in enumerate(spans)
    ]
    for load in loads:
        load.start()

    barrier = pltpu.get_barrier_semaphore()
    peers = [{"comp": 2 * chip + 1 - core, "pair": p}]
    peers += [{"comp": 2 * chip_at(m) + core, "pair": p} for m in range(1, chips)]
    peers += [{"comp": c, "pair": xor(p, k, pair_bits)} for k in range(1, pairs)]
    for peer in peers:
        pl.semaphore_signal(barrier, inc=1, device_id=peer, device_id_type=MESH)

    for load in loads[:comps]:
        load.wait()
    shape = (rows, comps * LANES)
    row = lax.broadcasted_iota(jnp.int32, shape, 0)
    col = lax.broadcasted_iota(jnp.int32, shape, 1)
    select = ((row // row_dev) * LANES + row % row_dev == col).astype(F32).astype(BF16)
    picked = jnp.concatenate([d_v[:, b * width : b * width + LANES] for b in range(comps)], axis=1)
    turned = lax.dot_general(select, picked, (((1,), (1,)), ((), ())), preferred_element_type=F32)
    per = block_len // LANES
    for i in range(per):
        cols = slice(i * LANES, (i + 1) * LANES)
        panel[p, :, cols] = (turned[:, cols] * w_ref[pl.ds(c * per + i, 1), :]).astype(BF16)

    pl.semaphore_wait(barrier, len(peers))

    def panel_copy(k, source):
        return pltpu.make_async_remote_copy(
            src_ref=panel.at[source],
            dst_ref=panel.at[source],
            send_sem=pan_s.at[k - 1],
            recv_sem=pan_r.at[k - 1],
            device_id={"comp": c, "pair": xor(p, k, pair_bits)},
            device_id_type=MESH,
        )

    for k in range(1, pairs):
        panel_copy(k, p).start()

    def core_copy(k, m):
        return pltpu.make_async_remote_copy(
            src_ref=core_out.at[k, m],
            dst_ref=core_in.at[k, m],
            send_sem=core_s.at[k, m],
            recv_sem=core_r.at[k, m],
            device_id={"comp": 2 * chip + 1 - core, "pair": p},
            device_id_type=MESH,
        )

    def chip_copy(k, m):
        return pltpu.make_async_remote_copy(
            src_ref=chip_out.at[k, m - 1],
            dst_ref=chip_in.at[k, m - 1],
            send_sem=chip_s.at[k, m - 1],
            recv_sem=chip_r.at[k, m - 1],
            device_id={"comp": 2 * chip_at(m) + core, "pair": p},
            device_id_type=MESH,
        )

    table = val_ref.shape
    place = lax.broadcasted_iota(jnp.int32, table, 0) * LANES
    place = place + lax.broadcasted_iota(jnp.int32, table, 1)
    tile = (row_dev, LANES)
    on_row = lax.broadcasted_iota(jnp.int32, tile, 0)
    on_col = lax.broadcasted_iota(jnp.int32, tile, 1)
    diagonal = jnp.zeros(tile, F32)
    for j in range(row_dev):
        up = jnp.where(place == list_ref[j, 1], cond_ref[...], 0.0)
        down = jnp.where(place == list_ref[j, 0], val_ref[...], 0.0)
        energy = jnp.sum(up, axis=(0, 1), keepdims=True) - jnp.sum(down, axis=(0, 1), keepdims=True)
        diagonal = jnp.where((on_row == j) & (on_col == j), energy, diagonal)

    for load in loads[comps:]:
        load.wait()

    def block(lhs, b):
        start = pl.multiple_of(b * width, width)
        return jnp.dot(lhs, d_v[:, pl.ds(start, width)], preferred_element_type=F32)

    def reduce(k):
        s = xor(p, k, pair_bits)
        total = own[k]
        for m in range(1, chips):
            chip_copy(k, m).wait_recv()
            total = total + chip_in[k, m - 1].astype(F32)
        for b in range(comps):
            at = pl.ds(pl.multiple_of((b * pairs + s) * row_dev, row_dev), row_dev)
            for t in range(width // TILE):
                cols = slice(t * TILE, (t + 1) * TILE)
                factor = 2.0 * mask_ref[t, b].astype(F32)
                acc[at, cols] = total[b * row_dev : (b + 1) * row_dev, cols] * factor

    def phase(k, carry):
        s = xor(p, k, pair_bits)

        @pl.when(k > 0)
        def _():
            panel_copy(k, s).wait_recv()

        lhs = panel[s]
        order = list(range(1, chips)) + [0]
        for m in order:
            core_out[k, m] = block(lhs, 2 * chip_at(m) + 1 - core).astype(BF16)
            core_copy(k, m).start()
        for m in order:
            part = block(lhs, 2 * chip_at(m) + core)
            core_copy(k, m).wait_recv()
            part = part + core_in[k, m].astype(F32)
            if m:
                chip_out[k, m - 1] = part.astype(BF16)
                chip_copy(k, m).start()
            else:
                own[k] = part

        @pl.when(k > 0)
        def _():
            reduce(k - 1)

        return carry

    lax.fori_loop(0, pairs, phase, 0)
    reduce(pairs - 1)

    at = pl.ds(pl.multiple_of((c * pairs + p) * row_dev, row_dev), row_dev)
    acc[at, :LANES] = acc[at, :LANES] + diagonal
    out_ref[...] = acc[...].T

    for k in range(1, pairs):
        panel_copy(k, p).wait_send()

    def drain(k, carry):
        for m in range(chips):
            core_copy(k, m).wait_send()
            if m:
                chip_copy(k, m).wait_send()
        return carry

    lax.fori_loop(0, pairs, drain, 0)


def per_device(densities, coulomb, pair_list, valence_energy, conduction_energy, tile_mask):
    comps = lax.axis_size("comp")
    pairs = lax.axis_size("pair")
    chips = comps // 2
    block_len, columns = densities.shape
    width = columns // comps
    row_dev = pair_list.shape[0]
    rows = comps * row_dev
    window = rows * pairs
    dma = pltpu.SemaphoreType.DMA
    vmem = pl.BlockSpec(memory_space=pltpu.VMEM)
    smem = pl.BlockSpec(memory_space=pltpu.SMEM)
    return pl.pallas_call(
        functools.partial(kernel, comps, pairs, row_dev),
        out_shape=jax.ShapeDtypeStruct((width, window), F32),
        in_specs=[pl.BlockSpec(memory_space=pl.ANY), vmem, smem, vmem, vmem, smem],
        out_specs=vmem,
        scratch_shapes=[
            pltpu.VMEM((block_len, columns), BF16),
            pltpu.VMEM((pairs, rows, block_len), BF16),
            pltpu.VMEM((pairs, rows, width), F32),
            pltpu.VMEM((pairs, chips, rows, width), BF16),
            pltpu.VMEM((pairs, chips, rows, width), BF16),
            pltpu.VMEM((pairs, chips - 1, rows, width), BF16),
            pltpu.VMEM((pairs, chips - 1, rows, width), BF16),
            pltpu.VMEM((window, width), F32),
            dma((2 * comps,)),
            dma((pairs - 1,)),
            dma((pairs - 1,)),
            dma((pairs, chips)),
            dma((pairs, chips)),
            dma((pairs, chips - 1)),
            dma((pairs, chips - 1)),
        ],
        compiler_params=pltpu.CompilerParams(
            collective_id=0, has_side_effects=True, vmem_limit_bytes=56 * 2**20
        ),
        cost_estimate=pl.CostEstimate(
            flops=2 * block_len * columns * window,
            bytes_accessed=2 * block_len * columns + 4 * width * window,
            transcendentals=0,
        ),
    )(
        densities,
        coulomb.reshape(-1, LANES),
        pair_list,
        valence_energy.reshape(-1, LANES),
        conduction_energy.reshape(-1, LANES),
        tile_mask,
    )


def solution(mesh):
    return jax.shard_map(
        per_device,
        mesh=mesh,
        in_specs=(
            P("comp", "pair"),
            P(),
            P(("comp", "pair"), None),
            P(),
            P(),
            P(("pair", "comp"), None),
        ),
        out_specs=P(("pair", "comp"), None),
        check_vma=False,
    )
```

time: 109 us -> 32.4 us (0.30)
  waiting for transfers between devices: 52.9 us -> 0 us
  Pallas kernels: 0 us -> 28.9 us
  blocking collectives: 17.4 us -> 0 us
  between operations: 13.5 us -> 0.01 us
  local copies, waits for them, and re-layouts: 14.4 us -> 3.21 us
  matrix products: 7.71 us -> 0 us
  other arithmetic: 2.39 us -> 0 us
    reduce_scatter x1 -> x0, waiting for transfers between devices: 52.8 us -> none  [per_device(): lax.psum_scatter(lax.dot_general(densities, panel, (((0,), (1,)), ((), ()...]
    pallas_call x0 -> x1, Pallas kernels: none -> 28.9 us  [per_device(): pl.pallas_call(functools.partial(kernel, comps, pairs, row_dev), out_shap...]
    all_gather x1 -> x0, blocking collectives: 17.4 us -> none  [per_device(): gathered = lax.all_gather(local_panel, 'pair', axis=1, tiled=True)]
    unnamed x9 -> x2, local copies, waits for them, and re-layouts: 12 us -> 3.21 us
    dot_general x1 -> x0, matrix products: 7.71 us -> none  [per_device(): lax.dot_general(densities, panel, (((0,), (1,)), ((), ())), preferred_ele...]
    add x2 -> x0, local copies, waits for them, and re-layouts: 1.46 us -> none  [per_device(): return masked + placed]
    mul x1 -> x0, other arithmetic: 1.13 us -> none  [per_device(): masked = 2.0 * masked.reshape(pair_dev, window)]
  transfers between devices with their start and end apart: 1 -> 0, of which waited for: 1 -> 0; matrix products, arithmetic and copies ran while one was open for 0% -> 0% of each run, Pallas kernels for 0% -> 0%
where the time goes in v1:
time: 32.4 us; the launch traced here: 32.1 us
  Pallas kernels  28.9 us (89%)
  local copies, waits for them, and re-layouts  3.21 us (10%)
    pallas_call x1, Pallas kernels, per_device(): pl.pallas_call(functools.partial(kernel, comps, pairs, row_dev), out_shap...  28.9 us
    unnamed x2, local copies, waits for them, and re-layouts  3.21 us

profile of v1, /device:TPU:0, one launch (start us, length us, event | category | flops | bytes accessed | tf_op | source)
XLA Modules:
  0.0 32.1 jit_solution(13565576768229099048)
XLA Ops:
  0.0 1.3 %copy.7.list_ref = s32[8,2]{1,0:T(8,128)} copy(s32[8,2]{0,1:T(2,128)} %param.8) | data formatting | bytes 128 | tf_op args[2]
  1.3 28.9 %shard_map.64 = f32[512,256]{1,0:T(8,128)} custom-call(bf16[1024,4096]{1,0:T(8,128)(2,1)} %d_hbm.1, f32[64,128]{1,0:T(8,128)} %bitcast.3, s32[8,2]{1,0:T(8,128)} %copy.7.list_ref, f32[32,128]{1,0:T(8,128)} %bitcast.4, f32[32,128]{1,0:T(8,128)} %bitcast.5, s32[4,8]{1,0:T(4,128)} %mask_ref.1), custom_call_target="tpu_custom_call" | custom-call | flops 2147483648 | bytes 8912896 | tf_op jit(solution)/shard_map/pallas_call | solution.py:204
  30.2 1.9 %copy.9 = f32[512,256]{1,0:T(8,128)} copy(f32[512,256]{1,0:T(8,128)} %shard_map.64) | data formatting | bytes 1048576

commit v2 on v1

v2 whole, which is shorter than its diff:
```python
import functools

import jax
import jax.numpy as jnp
from jax import lax
from jax.experimental import pallas as pl
from jax.experimental.pallas import tpu as pltpu
from jax.sharding import PartitionSpec as P

TILE = 128
LANES = 128
GROUP = 2
MESH = pl.DeviceIdType.MESH
F32 = jnp.float32
BF16 = jnp.bfloat16


def xor(a, b, bits):
    out = 0
    for i in range(bits):
        x, y = (a // 2**i) % 2, (b // 2**i) % 2
        out = out + 2**i * (x + y - 2 * x * y)
    return out


def kernel(
    comps, pairs, row_dev, group,
    d_hbm, w_hbm, list_hbm, val_hbm, cond_hbm, mask_hbm, out_hbm,
    d_v, w_ref, list_ref, val_ref, cond_ref, mask_ref,
    panel, own, core_out, core_in, chip_out, chip_in, acc, out_v,
    load_sem, small_sem, out_sem, pan_s, pan_r, core_s, core_r, chip_s, chip_r,
):
    c = lax.axis_index("comp")
    p = lax.axis_index("pair")
    chips = comps // 2
    chip_bits = chips.bit_length() - 1
    pair_bits = pairs.bit_length() - 1
    core, chip = c % 2, c // 2
    block_len = d_v.shape[0]
    width = d_v.shape[1] // comps
    rows = comps * row_dev
    groups = pairs // group

    def chip_at(m):
        return xor(chip, m, chip_bits)

    spans = [(b * width, LANES) for b in range(comps)]
    spans += [(b * width + LANES, width - LANES) for b in range(comps)]
    loads = [
        pltpu.make_async_copy(
            d_hbm.at[:, pl.ds(at, size)], d_v.at[:, pl.ds(at, size)], load_sem.at[i]
        )
        for i, (at, size) in enumerate(spans)
    ]
    small = [
        pltpu.make_async_copy(source, target, small_sem.at[i])
        for i, (source, target) in enumerate(
            [
                (w_hbm, w_ref),
                (list_hbm, list_ref),
                (val_hbm, val_ref),
                (cond_hbm, cond_ref),
                (mask_hbm, mask_ref),
            ]
        )
    ]
    for load in loads[:comps] + small + loads[comps:]:
        load.start()

    barrier = pltpu.get_barrier_semaphore()
    peers = [{"comp": 2 * chip + 1 - core, "pair": p}]
    peers += [{"comp": 2 * chip_at(m) + core, "pair": p} for m in range(1, chips)]
    peers += [{"comp": c, "pair": xor(p, k, pair_bits)} for k in range(1, pairs)]
    for peer in peers:
        pl.semaphore_signal(barrier, inc=1, device_id=peer, device_id_type=MESH)

    shape = (rows, comps * LANES)
    row = lax.broadcasted_iota(jnp.int32, shape, 0)
    col = lax.broadcasted_iota(jnp.int32, shape, 1)
    select = ((row // row_dev) * LANES + row % row_dev == col).astype(F32).astype(BF16)
    for load in loads[:comps] + small[:1]:
        load.wait()
    picked = jnp.concatenate([d_v[:, b * width : b * width + LANES] for b in range(comps)], axis=1)
    turned = lax.dot_general(select, picked, (((1,), (1,)), ((), ())), preferred_element_type=F32)
    per = block_len // LANES
    for i in range(per):
        cols = slice(i * LANES, (i + 1) * LANES)
        panel[0, :, cols] = (turned[:, cols] * w_ref[pl.ds(c * per + i, 1), :]).astype(BF16)

    pl.semaphore_wait(barrier, len(peers))

    def panel_copy(k):
        return pltpu.make_async_remote_copy(
            src_ref=panel.at[0],
            dst_ref=panel.at[k],
            send_sem=pan_s.at[k - 1],
            recv_sem=pan_r.at[k - 1],
            device_id={"comp": c, "pair": xor(p, k, pair_bits)},
            device_id_type=MESH,
        )

    for k in range(1, pairs):
        panel_copy(k).start()

    def core_copy(g, m):
        return pltpu.make_async_remote_copy(
            src_ref=core_out.at[g, m],
            dst_ref=core_in.at[g, m],
            send_sem=core_s.at[g, m],
            recv_sem=core_r.at[g, m],
            device_id={"comp": 2 * chip + 1 - core, "pair": p},
            device_id_type=MESH,
        )

    def chip_copy(g, m):
        return pltpu.make_async_remote_copy(
            src_ref=chip_out.at[g, m - 1],
            dst_ref=chip_in.at[g, m - 1],
            send_sem=chip_s.at[g, m - 1],
            recv_sem=chip_r.at[g, m - 1],
            device_id={"comp": 2 * chip_at(m) + core, "pair": p},
            device_id_type=MESH,
        )

    for load in small[1:]:
        load.wait()
    table = val_ref.shape
    place = lax.broadcasted_iota(jnp.int32, table, 0) * LANES
    place = place + lax.broadcasted_iota(jnp.int32, table, 1)
    tile = (row_dev, LANES)
    on_row = lax.broadcasted_iota(jnp.int32, tile, 0)
    on_col = lax.broadcasted_iota(jnp.int32, tile, 1)
    diagonal = jnp.zeros(tile, F32)
    for j in range(row_dev):
        up = jnp.where(place == list_ref[1, j], cond_ref[...], 0.0)
        down = jnp.where(place == list_ref[0, j], val_ref[...], 0.0)
        energy = jnp.sum(up, axis=(0, 1), keepdims=True) - jnp.sum(down, axis=(0, 1), keepdims=True)
        diagonal = jnp.where((on_row == j) & (on_col == j), energy, diagonal)

    for load in loads[comps:]:
        load.wait()

    def block(lhs, b):
        start = pl.multiple_of(b * width, width)
        return jnp.dot(lhs, d_v[:, pl.ds(start, width)], preferred_element_type=F32)

    def reduce(g):
        total = own[g]
        for m in range(1, chips):
            chip_copy(g, m).wait_recv()
            total = total + chip_in[g, m - 1].astype(F32)
        for i in range(group):
            s = xor(p, g * group + i, pair_bits)
            for b in range(comps):
                at = pl.ds(pl.multiple_of((b * pairs + s) * row_dev, row_dev), row_dev)
                first = i * rows + b * row_dev
                for t in range(width // TILE):
                    cols = slice(t * TILE, (t + 1) * TILE)
                    factor = 2.0 * mask_ref[t, b].astype(F32)
                    acc[at, cols] = total[first : first + row_dev, cols] * factor

    order = list(range(chips - 1, 0, -1)) + [0]
    steps = [(m, True) for m in order[:2]]
    for i, m in enumerate(order):
        steps.append((m, False))
        if i + 2 < chips:
            steps.append((order[i + 2], True))

    def phase(g, carry):
        for i in range(group):
            if i:
                panel_copy(g * group + i).wait_recv()
            else:

                @pl.when(g > 0)
                def _():
                    panel_copy(g * group).wait_recv()

        lhs = panel[pl.ds(g * group, group)].reshape(group * rows, block_len)
        for m, away in steps:
            if away:
                core_out[g, m] = block(lhs, 2 * chip_at(m) + 1 - core).astype(BF16)
                core_copy(g, m).start()
                continue
            part = block(lhs, 2 * chip_at(m) + core)
            core_copy(g, m).wait_recv()
            part = part + core_in[g, m].astype(F32)
            if m:
                chip_out[g, m - 1] = part.astype(BF16)
                chip_copy(g, m).start()
            else:
                own[g] = part

        @pl.when(g > 0)
        def _():
            reduce(g - 1)

        return carry

    lax.fori_loop(0, groups, phase, 0)
    reduce(groups - 1)

    at = pl.ds(pl.multiple_of((c * pairs + p) * row_dev, row_dev), row_dev)
    acc[at, :LANES] = acc[at, :LANES] + diagonal
    stores = []
    for t in range(width // TILE):
        cut = pl.ds(t * TILE, TILE)
        out_v[cut, :] = acc[:, t * TILE : (t + 1) * TILE].T
        stores.append(pltpu.make_async_copy(out_v.at[cut], out_hbm.at[cut], out_sem.at[t]))
        stores[-1].start()

    for k in range(1, pairs):
        panel_copy(k).wait_send()

    def drain(g, carry):
        for m in range(chips):
            core_copy(g, m).wait_send()
            if m:
                chip_copy(g, m).wait_send()
        return carry

    lax.fori_loop(0, groups, drain, 0)
    for store in stores:
        store.wait()


def per_device(densities, coulomb, pair_list, valence_energy, conduction_energy, tile_mask):
    comps = lax.axis_size("comp")
    pairs = lax.axis_size("pair")
    chips = comps // 2
    block_len, columns = densities.shape
    width = columns // comps
    row_dev = pair_list.shape[0]
    rows = comps * row_dev
    window = rows * pairs
    group = GROUP
    groups = pairs // group
    dma = pltpu.SemaphoreType.DMA
    operands = (
        densities,
        coulomb.reshape(-1, LANES),
        pair_list.T,
        valence_energy.reshape(-1, LANES),
        conduction_energy.reshape(-1, LANES),
        tile_mask,
    )
    _, w, pair, val, cond, mask = operands
    return pl.pallas_call(
        functools.partial(kernel, comps, pairs, row_dev, group),
        out_shape=jax.ShapeDtypeStruct((width, window), F32),
        in_specs=[pl.BlockSpec(memory_space=pl.ANY)] * 6,
        out_specs=pl.BlockSpec(memory_space=pl.ANY),
        scratch_shapes=[
            pltpu.VMEM((block_len, columns), BF16),
            pltpu.VMEM(w.shape, F32),
            pltpu.SMEM(pair.shape, jnp.int32),
            pltpu.VMEM(val.shape, F32),
            pltpu.VMEM(cond.shape, F32),
            pltpu.SMEM(mask.shape, jnp.int32),
            pltpu.VMEM((pairs, rows, block_len), BF16),
            pltpu.VMEM((groups, group * rows, width), F32),
            pltpu.VMEM((groups, chips, group * rows, width), BF16),
            pltpu.VMEM((groups, chips, group * rows, width), BF16),
            pltpu.VMEM((groups, chips - 1, group * rows, width), BF16),
            pltpu.VMEM((groups, chips - 1, group * rows, width), BF16),
            pltpu.VMEM((window, width), F32),
            pltpu.VMEM((width, window), F32),
            dma((2 * comps,)),
            dma((5,)),
            dma((width // TILE,)),
            dma((pairs - 1,)),
            dma((pairs - 1,)),
            dma((groups, chips)),
            dma((groups, chips)),
            dma((groups, chips - 1)),
            dma((groups, chips - 1)),
        ],
        compiler_params=pltpu.CompilerParams(
            collective_id=0, has_side_effects=True, vmem_limit_bytes=56 * 2**20
        ),
        cost_estimate=pl.CostEstimate(
            flops=2 * block_len * columns * window,
            bytes_accessed=2 * block_len * columns + 4 * width * window,
            transcendentals=0,
        ),
    )(*operands)


def solution(mesh):
    return jax.shard_map(
        per_device,
        mesh=mesh,
        in_specs=(
            P("comp", "pair"),
            P(),
            P(("comp", "pair"), None),
            P(),
            P(),
            P(("pair", "comp"), None),
        ),
        out_specs=P(("pair", "comp"), None),
        check_vma=False,
    )
```

time: 32.4 us -> 31.6 us (0.975)
  local copies, waits for them, and re-layouts: 3.21 us -> 1.87 us
  Pallas kernels: 28.9 us -> 29.6 us
    unnamed x2 -> x1, local copies, waits for them, and re-layouts: 3.21 us -> 1.87 us
    pallas_call x1, Pallas kernels: 28.9 us -> 29.6 us  [per_device(): pl.pallas_call(functools.partial(kernel, comps, pairs, row_dev, group), o...]
where the time goes in v2:
time: 31.6 us; the launch traced here: 31.4 us
  Pallas kernels  29.6 us (94%)
  local copies, waits for them, and re-layouts  1.87 us (6%)
    pallas_call x1, Pallas kernels, per_device(): pl.pallas_call(functools.partial(kernel, comps, pairs, row_dev, group), o...  29.6 us
    unnamed x1, local copies, waits for them, and re-layouts  1.87 us

profile of v2, /device:TPU:0, one launch (start us, length us, event | category | flops | bytes accessed | tf_op | source)
XLA Modules:
  0.0 31.4 jit_solution(7317561863777874156)
XLA Ops:
  0.0 29.6 %shard_map.64 = f32[512,256]{1,0:T(8,128)} custom-call(bf16[1024,4096]{1,0:T(8,128)(2,1)} %d_hbm.1, f32[64,128]{1,0:T(8,128)} %bitcast.4, s32[2,8]{1,0:T(2,128)} %bitcast.7, f32[32,128]{1,0:T(8,128)} %bitcast.5, f32[32,128]{1,0:T(8,128)} %bitcast.6, s32[4,8]{1,0:T(4,128)} %mask_hbm.1), custom_call_target="tpu_custom_call" | custom-call | flops 2147483648 | bytes 8912896 | tf_op jit(solution)/shard_map/pallas_call | solution.py:248
  29.6 1.9 %copy.8 = f32[512,256]{1,0:T(8,128)} copy(f32[512,256]{1,0:T(8,128)} %shard_map.64) | data formatting | bytes 1048576

commit v3 on v2

--- a/solution.py
+++ b/solution.py
@@ -9,7 +9,7 @@
 
 TILE = 128
 LANES = 128
-GROUP = 2
+GROUP = 1
 MESH = pl.DeviceIdType.MESH
 F32 = jnp.float32
 BF16 = jnp.bfloat16

time: 31.6 us -> 31.5 us (level)
  no operation moved by 1% of the time
where the time goes in v3:
time: 31.5 us; the launch traced here: 31.3 us
  Pallas kernels  29.4 us (93%)
  local copies, waits for them, and re-layouts  1.87 us (6%)
    pallas_call x1, Pallas kernels, per_device(): pl.pallas_call(functools.partial(kernel, comps, pairs, row_dev, group), o...  29.4 us
    unnamed x1, local copies, waits for them, and re-layouts  1.87 us

profile of v3, /device:TPU:0, one launch (start us, length us, event | category | flops | bytes accessed | tf_op | source)
XLA Modules:
  0.0 31.3 jit_solution(10381443589241660562)
XLA Ops:
  0.0 29.4 %shard_map.64 = f32[512,256]{1,0:T(8,128)} custom-call(bf16[1024,4096]{1,0:T(8,128)(2,1)} %d_hbm.1, f32[64,128]{1,0:T(8,128)} %bitcast.4, s32[2,8]{1,0:T(2,128)} %bitcast.7, f32[32,128]{1,0:T(8,128)} %bitcast.5, f32[32,128]{1,0:T(8,128)} %bitcast.6, s32[4,8]{1,0:T(4,128)} %mask_hbm.1), custom_call_target="tpu_custom_call" | custom-call | flops 2147483648 | bytes 8912896 | tf_op jit(solution)/shard_map/pallas_call | solution.py:248
  29.4 1.9 %copy.8 = f32[512,256]{1,0:T(8,128)} copy(f32[512,256]{1,0:T(8,128)} %shard_map.64) | data formatting | bytes 1048576

commit v4 on v2

--- a/solution.py
+++ b/solution.py
@@ -10,6 +10,7 @@
 TILE = 128
 LANES = 128
 GROUP = 2
+HALVES = 2
 MESH = pl.DeviceIdType.MESH
 F32 = jnp.float32
 BF16 = jnp.bfloat16
@@ -28,7 +29,7 @@
     d_hbm, w_hbm, list_hbm, val_hbm, cond_hbm, mask_hbm, out_hbm,
     d_v, w_ref, list_ref, val_ref, cond_ref, mask_ref,
     panel, own, core_out, core_in, chip_out, chip_in, acc, out_v,
-    load_sem, small_sem, out_sem, pan_s, pan_r, core_s, core_r, chip_s, chip_r,
+    load_sem, small_sem, out_sem, pan_s, pan_r, pass_s, core_s, core_r, chip_s, chip_r,
 ):
     c = lax.axis_index("comp")
     p = lax.axis_index("pair")
@@ -40,6 +41,8 @@
     width = d_v.shape[1] // comps
     rows = comps * row_dev
     groups = pairs // group
+    half = block_len // HALVES
+    middle = ((p + 1) // 2) % 2 == 1
 
     def chip_at(m):
         return xor(chip, m, chip_bits)
@@ -85,22 +88,36 @@
     per = block_len // LANES
     for i in range(per):
         cols = slice(i * LANES, (i + 1) * LANES)
-        panel[0, :, cols] = (turned[:, cols] * w_ref[pl.ds(c * per + i, 1), :]).astype(BF16)
+        h, at = divmod(i * LANES, half)
+        weighted = turned[:, cols] * w_ref[pl.ds(c * per + i, 1), :]
+        panel[h, 0, :, at : at + LANES] = weighted.astype(BF16)
 
     pl.semaphore_wait(barrier, len(peers))
 
-    def panel_copy(k):
+    def panel_copy(k, h, source=0, to=None, sem=None):
         return pltpu.make_async_remote_copy(
-            src_ref=panel.at[0],
-            dst_ref=panel.at[k],
-            send_sem=pan_s.at[k - 1],
-            recv_sem=pan_r.at[k - 1],
-            device_id={"comp": c, "pair": xor(p, k, pair_bits)},
+            src_ref=panel.at[h, source],
+            dst_ref=panel.at[h, k],
+            send_sem=pan_s.at[k - 1, h] if sem is None else sem,
+            recv_sem=pan_r.at[k - 1, h],
+            device_id={"comp": c, "pair": xor(p, k if to is None else to, pair_bits)},
             device_id_type=MESH,
         )
 
-    for k in range(1, pairs):
-        panel_copy(k).start()
+    def pass_on(source, h):
+        to, slot = {3: (1, 2), 1: (3, 2), 2: (1, 3)}[source]
+        return panel_copy(slot, h, source, to, pass_s.at[source - 1, h])
+
+    for h in range(HALVES):
+        panel_copy(1, h).start()
+
+        @pl.when(middle)
+        def _():
+            panel_copy(3, h).start()
+
+    for k in range(4, pairs):
+        for h in range(HALVES):
+            panel_copy(k, h).start()
 
     def core_copy(g, m):
         return pltpu.make_async_remote_copy(
@@ -144,20 +161,18 @@
         start = pl.multiple_of(b * width, width)
         return jnp.dot(lhs, d_v[:, pl.ds(start, width)], preferred_element_type=F32)
 
-    def reduce(g):
-        total = own[g]
+    def reduce(g, t):
+        cols = slice(t * TILE, (t + 1) * TILE)
+        total = own[g, :, cols]
         for m in range(1, chips):
-            chip_copy(g, m).wait_recv()
-            total = total + chip_in[g, m - 1].astype(F32)
+            total = total + chip_in[g, m - 1, :, cols].astype(F32)
         for i in range(group):
             s = xor(p, g * group + i, pair_bits)
             for b in range(comps):
                 at = pl.ds(pl.multiple_of((b * pairs + s) * row_dev, row_dev), row_dev)
                 first = i * rows + b * row_dev
-                for t in range(width // TILE):
-                    cols = slice(t * TILE, (t + 1) * TILE)
-                    factor = 2.0 * mask_ref[t, b].astype(F32)
-                    acc[at, cols] = total[first : first + row_dev, cols] * factor
+                factor = 2.0 * mask_ref[t, b].astype(F32)
+                acc[at, cols] = total[first : first + row_dev] * factor
 
     order = list(range(chips - 1, 0, -1)) + [0]
     steps = [(m, True) for m in order[:2]]
@@ -167,16 +182,37 @@
             steps.append((order[i + 2], True))
 
     def phase(g, carry):
-        for i in range(group):
-            if i:
-                panel_copy(g * group + i).wait_recv()
-            else:
-
-                @pl.when(g > 0)
-                def _():
-                    panel_copy(g * group).wait_recv()
-
-        lhs = panel[pl.ds(g * group, group)].reshape(group * rows, block_len)
+        @pl.when((g == 0) & middle)
+        def _():
+            for h in range(HALVES):
+                for k in (3, 1):
+                    panel_copy(k, h).wait_recv()
+                    pass_on(k, h).start()
+
+        @pl.when((g == 0) & jnp.logical_not(middle))
+        def _():
+            for h in range(HALVES):
+                panel_copy(1, h).wait_recv()
+
+        @pl.when((g == 1) & jnp.logical_not(middle))
+        def _():
+            for h in range(HALVES):
+                panel_copy(2, h).wait_recv()
+                panel_copy(3, h).wait_recv()
+
+        @pl.when(g > 1)
+        def _():
+            for i in range(group):
+                for h in range(HALVES):
+                    panel_copy(g * group + i, h).wait_recv()
+
+        lhs = jnp.concatenate(
+            [
+                panel[h, pl.ds(g * group, group)].reshape(group * rows, half)
+                for h in range(HALVES)
+            ],
+            axis=1,
+        )
         for m, away in steps:
             if away:
                 core_out[g, m] = block(lhs, 2 * chip_at(m) + 1 - core).astype(BF16)
@@ -191,26 +227,47 @@
             else:
                 own[g] = part
 
+        @pl.when((g == 0) & middle)
+        def _():
+            for h in range(HALVES):
+                panel_copy(2, h).wait_recv()
+                pass_on(2, h).start()
+
         @pl.when(g > 0)
         def _():
-            reduce(g - 1)
+            for m in range(1, chips):
+                chip_copy(g - 1, m).wait_recv()
+            for t in range(width // TILE):
+                reduce(g - 1, t)
 
         return carry
 
     lax.fori_loop(0, groups, phase, 0)
-    reduce(groups - 1)
+    for m in range(chips - 1, 0, -1):
+        chip_copy(groups - 1, m).wait_recv()
 
     at = pl.ds(pl.multiple_of((c * pairs + p) * row_dev, row_dev), row_dev)
-    acc[at, :LANES] = acc[at, :LANES] + diagonal
     stores = []
     for t in range(width // TILE):
+        reduce(groups - 1, t)
+        if t == 0:
+            acc[at, :LANES] = acc[at, :LANES] + diagonal
         cut = pl.ds(t * TILE, TILE)
         out_v[cut, :] = acc[:, t * TILE : (t + 1) * TILE].T
         stores.append(pltpu.make_async_copy(out_v.at[cut], out_hbm.at[cut], out_sem.at[t]))
         stores[-1].start()
 
-    for k in range(1, pairs):
-        panel_copy(k).wait_send()
+    for h in range(HALVES):
+        panel_copy(1, h).wait_send()
+
+        @pl.when(middle)
+        def _():
+            panel_copy(3, h).wait_send()
+            for k in (3, 1, 2):
+                pass_on(k, h).wait_send()
+
+        for k in range(4, pairs):
+            panel_copy(k, h).wait_send()
 
     def drain(g, carry):
         for m in range(chips):
@@ -257,7 +314,7 @@
             pltpu.VMEM(val.shape, F32),
             pltpu.VMEM(cond.shape, F32),
             pltpu.SMEM(mask.shape, jnp.int32),
-            pltpu.VMEM((pairs, rows, block_len), BF16),
+            pltpu.VMEM((HALVES, pairs, rows, block_len // HALVES), BF16),
             pltpu.VMEM((groups, group * rows, width), F32),
             pltpu.VMEM((groups, chips, group * rows, width), BF16),
             pltpu.VMEM((groups, chips, group * rows, width), BF16),
@@ -268,8 +325,9 @@
             dma((2 * comps,)),
             dma((5,)),
             dma((width // TILE,)),
-            dma((pairs - 1,)),
-            dma((pairs - 1,)),
+            dma((pairs - 1, HALVES)),
+            dma((pairs - 1, HALVES)),
+            dma((3, HALVES)),
             dma((groups, chips)),
             dma((groups, chips)),
             dma((groups, chips - 1)),

time: 31.6 us -> 32.3 us (1.022)
  Pallas kernels: 29.6 us -> 30.2 us
    pallas_call x1, Pallas kernels: 29.6 us -> 30.2 us  [per_device(): pl.pallas_call(functools.partial(kernel, comps, pairs, row_dev, group), o...]
where the time goes in v4:
time: 32.3 us; the launch traced here: 32.1 us
  Pallas kernels  30.2 us (93%)
  local copies, waits for them, and re-layouts  1.87 us (6%)
    pallas_call x1, Pallas kernels, per_device(): pl.pallas_call(functools.partial(kernel, comps, pairs, row_dev, group), o...  30.2 us
    unnamed x1, local copies, waits for them, and re-layouts  1.87 us

profile of v4, /device:TPU:0, one launch (start us, length us, event | category | flops | bytes accessed | tf_op | source)
XLA Modules:
  0.0 32.1 jit_solution(2073292193511929063)
XLA Ops:
  0.0 30.2 %shard_map.64 = f32[512,256]{1,0:T(8,128)} custom-call(bf16[1024,4096]{1,0:T(8,128)(2,1)} %d_hbm.1, f32[64,128]{1,0:T(8,128)} %bitcast.4, s32[2,8]{1,0:T(2,128)} %bitcast.7, f32[32,128]{1,0:T(8,128)} %bitcast.5, f32[32,128]{1,0:T(8,128)} %bitcast.6, s32[4,8]{1,0:T(4,128)} %mask_hbm.1), custom_call_target="tpu_custom_call" | custom-call | flops 2147483648 | bytes 8912896 | tf_op jit(solution)/shard_map/pallas_call | solution.py:305
  30.2 1.9 %copy.8 = f32[512,256]{1,0:T(8,128)} copy(f32[512,256]{1,0:T(8,128)} %shard_map.64) | data formatting | bytes 1048576

commit v5 on v4

--- a/solution.py
+++ b/solution.py
@@ -105,8 +105,8 @@
         )
 
     def pass_on(source, h):
-        to, slot = {3: (1, 2), 1: (3, 2), 2: (1, 3)}[source]
-        return panel_copy(slot, h, source, to, pass_s.at[source - 1, h])
+        to, slot = {3: (1, 2), 2: (1, 3)}[source]
+        return panel_copy(slot, h, source, to, pass_s.at[source - 2, h])
 
     for h in range(HALVES):
         panel_copy(1, h).start()
@@ -114,6 +114,11 @@
         @pl.when(middle)
         def _():
             panel_copy(3, h).start()
+
+    @pl.when(jnp.logical_not(middle))
+    def _():
+        for h in range(HALVES):
+            panel_copy(2, h).start()
 
     for k in range(4, pairs):
         for h in range(HALVES):
@@ -176,18 +181,20 @@
 
     order = list(range(chips - 1, 0, -1)) + [0]
     steps = [(m, True) for m in order[:2]]
-    for i, m in enumerate(order):
+    for i, m in enumerate(order[:-1]):
         steps.append((m, False))
-        if i + 2 < chips:
+        if i + 3 < chips:
             steps.append((order[i + 2], True))
+    steps += [(0, True), (0, False)]
 
     def phase(g, carry):
         @pl.when((g == 0) & middle)
         def _():
             for h in range(HALVES):
-                for k in (3, 1):
-                    panel_copy(k, h).wait_recv()
-                    pass_on(k, h).start()
+                panel_copy(3, h).wait_recv()
+                pass_on(3, h).start()
+            for h in range(HALVES):
+                panel_copy(1, h).wait_recv()
 
         @pl.when((g == 0) & jnp.logical_not(middle))
         def _():
@@ -213,7 +220,15 @@
             ],
             axis=1,
         )
-        for m, away in steps:
+        for step, (m, away) in enumerate(steps):
+            for h in range(HALVES):
+                if step == 3 + 2 * h:
+
+                    @pl.when((g == 0) & middle)
+                    def _():
+                        panel_copy(2, h).wait_recv()
+                        pass_on(2, h).start()
+
             if away:
                 core_out[g, m] = block(lhs, 2 * chip_at(m) + 1 - core).astype(BF16)
                 core_copy(g, m).start()
@@ -227,12 +242,6 @@
             else:
                 own[g] = part
 
-        @pl.when((g == 0) & middle)
-        def _():
-            for h in range(HALVES):
-                panel_copy(2, h).wait_recv()
-                pass_on(2, h).start()
-
         @pl.when(g > 0)
         def _():
             for m in range(1, chips):
@@ -263,8 +272,12 @@
         @pl.when(middle)
         def _():
             panel_copy(3, h).wait_send()
-            for k in (3, 1, 2):
+            for k in (3, 2):
                 pass_on(k, h).wait_send()
+
+        @pl.when(jnp.logical_not(middle))
+        def _():
+            panel_copy(2, h).wait_send()
 
         for k in range(4, pairs):
             panel_copy(k, h).wait_send()
@@ -327,7 +340,7 @@
             dma((width // TILE,)),
             dma((pairs - 1, HALVES)),
             dma((pairs - 1, HALVES)),
-            dma((3, HALVES)),
+            dma((2, HALVES)),
             dma((groups, chips)),
             dma((groups, chips)),
             dma((groups, chips - 1)),

time: 32.3 us -> 30.9 us (0.957)
  Pallas kernels: 30.2 us -> 28.9 us
    pallas_call x1, Pallas kernels: 30.2 us -> 28.9 us  [per_device(): pl.pallas_call(functools.partial(kernel, comps, pairs, row_dev, group), o...]
where the time goes in v5:
time: 30.9 us; the launch traced here: 30.8 us
  Pallas kernels  28.9 us (94%)
  local copies, waits for them, and re-layouts  1.87 us (6%)
    pallas_call x1, Pallas kernels, per_device(): pl.pallas_call(functools.partial(kernel, comps, pairs, row_dev, group), o...  28.9 us
    unnamed x1, local copies, waits for them, and re-layouts  1.87 us

profile of v5, /device:TPU:0, one launch (start us, length us, event | category | flops | bytes accessed | tf_op | source)
XLA Modules:
  0.0 30.8 jit_solution(2774818478211012715)
XLA Ops:
  0.0 28.9 %shard_map.64 = f32[512,256]{1,0:T(8,128)} custom-call(bf16[1024,4096]{1,0:T(8,128)(2,1)} %d_hbm.1, f32[64,128]{1,0:T(8,128)} %bitcast.4, s32[2,8]{1,0:T(2,128)} %bitcast.7, f32[32,128]{1,0:T(8,128)} %bitcast.5, f32[32,128]{1,0:T(8,128)} %bitcast.6, s32[4,8]{1,0:T(4,128)} %mask_hbm.1), custom_call_target="tpu_custom_call" | custom-call | flops 2147483648 | bytes 8912896 | tf_op jit(solution)/shard_map/pallas_call | solution.py:318
  28.9 1.9 %copy.8 = f32[512,256]{1,0:T(8,128)} copy(f32[512,256]{1,0:T(8,128)} %shard_map.64) | data formatting | bytes 1048576

commit v6 on v5

--- a/solution.py
+++ b/solution.py
@@ -77,13 +77,17 @@
     for peer in peers:
         pl.semaphore_signal(barrier, inc=1, device_id=peer, device_id_type=MESH)
 
-    shape = (rows, comps * LANES)
-    row = lax.broadcasted_iota(jnp.int32, shape, 0)
-    col = lax.broadcasted_iota(jnp.int32, shape, 1)
-    select = ((row // row_dev) * LANES + row % row_dev == col).astype(F32).astype(BF16)
+    row = lax.broadcasted_iota(jnp.int32, (rows, LANES), 0)
+    col = lax.broadcasted_iota(jnp.int32, (rows, LANES), 1)
+    select = (row == col).astype(F32).astype(BF16)
+    lane = lax.broadcasted_iota(jnp.int32, (block_len, LANES), 1) // row_dev
     for load in loads[:comps] + small[:1]:
         load.wait()
-    picked = jnp.concatenate([d_v[:, b * width : b * width + LANES] for b in range(comps)], axis=1)
+    packed = d_v[:, :LANES].astype(F32)
+    for b in range(1, comps):
+        moved = pltpu.roll(d_v[:, b * width : b * width + LANES].astype(F32), b * row_dev, 1)
+        packed = jnp.where(lane == b, moved, packed)
+    picked = packed.astype(BF16)
     turned = lax.dot_general(select, picked, (((1,), (1,)), ((), ())), preferred_element_type=F32)
     per = block_len // LANES
     for i in range(per):

time: 30.9 us -> 31 us (level)
  no operation moved by 1% of the time
where the time goes in v6:
time: 31 us; the launch traced here: 30.8 us
  Pallas kernels  29 us (94%)
  local copies, waits for them, and re-layouts  1.87 us (6%)
    pallas_call x1, Pallas kernels, per_device(): pl.pallas_call(functools.partial(kernel, comps, pairs, row_dev, group), o...  29 us
    unnamed x1, local copies, waits for them, and re-layouts  1.87 us

profile of v6, /device:TPU:0, one launch (start us, length us, event | category | flops | bytes accessed | tf_op | source)
XLA Modules:
  0.0 30.8 jit_solution(12311369429264967538)
XLA Ops:
  0.0 29.0 %shard_map.64 = f32[512,256]{1,0:T(8,128)} custom-call(bf16[1024,4096]{1,0:T(8,128)(2,1)} %d_hbm.1, f32[64,128]{1,0:T(8,128)} %bitcast.4, s32[2,8]{1,0:T(2,128)} %bitcast.7, f32[32,128]{1,0:T(8,128)} %bitcast.5, f32[32,128]{1,0:T(8,128)} %bitcast.6, s32[4,8]{1,0:T(4,128)} %mask_hbm.1), custom_call_target="tpu_custom_call" | custom-call | flops 2147483648 | bytes 8912896 | tf_op jit(solution)/shard_map/pallas_call | solution.py:322
  29.0 1.9 %copy.8 = f32[512,256]{1,0:T(8,128)} copy(f32[512,256]{1,0:T(8,128)} %shard_map.64) | data formatting | bytes 1048576
